TPU v7x, 128 devices: a whole 4x4x4 slice. The times are simulated.
128 devices in a mesh: req: 4 (over y), blk: 32 (over z, x, core).
Axes of the slice: x: 4, y: 4, z: 4, core: 2. Of those that a mesh axis runs over, the one named last changes fastest.
Arguments:
- queries: bfloat16 [4, 4096, 4096], P('req', 'blk'), may hold values from -12.5 to 12.5
- fresh_cache: bfloat16 [4, 4096, 1024], P('req', 'blk'), may hold values from -12.5 to 12.5
- page_store: bfloat16 [512, 32, 1024], P(('req', 'blk')), may hold values from -12.5 to 12.5
- page_table: int32 [4, 128], replicated, may hold values from 0 to 511, as said below
- prefix_lengths: int32 [4], replicated, may hold values from 819 to 4096, as said below
Outputs:
- attended: bfloat16 [4, 4096, 4096], P('req', 'blk')
- new_pages: bfloat16 [4, 4, 32, 32, 1024], P('req', None, 'blk')
Inputs may be any that keep to these rules, and one draw needn't show every extreme that they name: page_table[r, p] is the slot of page_store holding prefix page p of request r; all slots are distinct and cover the store; slot s holds a page of request (s % 4), so each block of 4 slots holds exactly one page of every request. `prefix_lengths`: some request has a prefix of exactly 4096 tokens.
All inputs are finite; a program needn't handle non-finite values.
Results may differ from a plain program's by a relative error of at most 0.0065.
Values may be sent and summed in bfloat16 or wider, within the bound.
A program may use at most 192 MiB of HBM per device.

v0:
```python
import functools
import math

import jax
import jax.numpy as jnp
from jax import lax
from jax.experimental import pallas as pl
from jax.experimental.pallas import tpu as pltpu
from jax.sharding import PartitionSpec as P

H = 32
KVH = 4
HD = 128
GROUP = H // KVH
TOK = 128
PAGE = 32
CHUNK = 1024
ROWS = GROUP * TOK
NEG = -1e30
SCALE = math.log2(math.e) / math.sqrt(HD)
MESH = pl.DeviceIdType.MESH
BLOCK = 256


def kernel(
    queries, fresh, pages, table, lengths, attended, written,
    kvx, raw, q_raw, q_two, acc, top, o_buf, limits,
    pg_send, pg_recv, fr_send, fr_recv, q_send, q_recv, o_send, o_recv,
    np_send, np_recv, pre_send, pre_recv, suf_send, suf_recv,
):
    y = lax.axis_index("req")
    blk = lax.axis_index("blk")
    z, x, c = blk // 8, (blk // 2) % 4, blk % 2

    def at(dy, dz, dx, dc):
        z2, x2 = lax.rem(z + dz, 4), lax.rem(x + dx, 4)
        c2 = 1 - c if dc else c
        return (lax.rem(y + dy, 4), z2 * 8 + x2 * 2 + c2)

    def remote(src, dst, send, recv, device):
        return pltpu.make_async_remote_copy(
            src_ref=src, dst_ref=dst, send_sem=send, recv_sem=recv,
            device_id=device, device_id_type=MESH,
        )

    right, left, sibling = at(0, 0, 1, 0), at(0, 0, 3, 0), at(0, 0, 0, 1)
    others = [(dy, dz) for dz in (0, 1, 3, 2) for dy in (0, 1, 3, 2) if dy or dz]
    greeted = [at(dy, dz, 0, 0) for dy, dz in others] + [right, left, sibling]
    barrier = pltpu.get_barrier_semaphore()
    for device in greeted:
        pl.semaphore_signal(barrier, inc=1, device_id=device, device_id_type=MESH)
    pl.semaphore_wait(barrier, len(greeted))

    def lanes(first, size=HD):
        return pl.ds(pl.multiple_of(first, HD), size)

    my_rows = pl.ds(pl.multiple_of((y * 4 + z) * PAGE, PAGE), PAGE)
    page_copies = []
    n = 0
    for dy, dz in others:
        y2, z2 = lax.rem(y + dy, 4), lax.rem(z + dz, 4)
        for plane in range(2):
            page_copies.append(remote(
                pages.at[y2, :, lanes(plane * 512 + z2 * HD)],
                raw.at[plane, 0, c, my_rows],
                pg_send.at[n], pg_recv, at(dy, dz, 0, 0),
            ))
            n += 1
    for copy in page_copies:
        copy.start()
    own_pages = [
        pltpu.make_async_copy(
            pages.at[y, :, lanes(plane * 512 + z * HD)], raw.at[plane, 0, c, my_rows], pg_recv
        )
        for plane in range(2)
    ]
    for copy in own_pages:
        copy.start()

    own_q = pltpu.make_async_copy(queries.at[0, :, lanes(z * ROWS, ROWS)], q_raw.at[z], q_recv.at[0])
    own_q.start()
    xc = x * 2 + c
    fresh_copies = []
    n = 0
    for dz in (1, 3, 2):
        z2 = lax.rem(z + dz, 4)
        for plane in range(2):
            fresh_copies.append(remote(
                fresh.at[0, :, lanes(plane * 512 + z2 * HD)],
                kvx.at[plane, 4 + z, xc],
                fr_send.at[n], fr_recv, at(0, dz, 0, 0),
            ))
            n += 1
    for copy in fresh_copies:
        copy.start()
    own_fresh = [
        pltpu.make_async_copy(
            fresh.at[0, :, lanes(plane * 512 + z * HD)], kvx.at[plane, 4 + z, xc], fr_recv
        )
        for plane in range(2)
    ]
    for copy in own_fresh:
        copy.start()
    q_copies = {}
    for k, dz in enumerate((1, 3, 2)):
        z2 = lax.rem(z + dz, 4)
        k_there = {1: 2, 3: 1, 2: 3}[dz]
        q_copies[k] = remote(
            queries.at[0, :, lanes(z2 * ROWS, ROWS)], q_raw.at[z],
            q_send.at[k], q_recv.at[k_there], at(0, dz, 0, 0),
        )
        q_copies[k].start()
    written_copies = []
    for k, dy in enumerate((1, 2, 3)):
        y2 = lax.rem(y + dy, 4)
        written_copies.append(remote(
            fresh.at[0, pl.ds(pl.multiple_of(y2 * PAGE, PAGE), PAGE)], written.at[0, y, 0],
            np_send.at[k], np_recv, at(dy, 0, 0, 0),
        ))
    own_written = pltpu.make_async_copy(
        fresh.at[0, pl.ds(pl.multiple_of(y * PAGE, PAGE), PAGE)], written.at[0, y, 0], np_recv
    )

    length = lengths[y]
    j = lax.broadcasted_iota(jnp.int32, (128, 128), 0)
    rel = j // 32
    x_of = lax.rem(x + jnp.where(rel == 0, 0, jnp.where(rel == 1, 3, jnp.where(rel == 2, 1, 2))), 4)
    c_of = (j // 16) % 2
    y_of, z_of = (j // 4) % 4, j % 4
    slot = 4 * (y_of * 32 + z_of * 8 + x_of * 2 + c_of) + y
    page = lax.broadcasted_iota(jnp.int32, (128, 128), 1)
    match = jnp.broadcast_to(table[pl.ds(y, 1), :], (128, 128)) == slot
    place = jnp.sum(jnp.where(match, page, 0).astype(jnp.float32), axis=1, keepdims=True)
    limits[...] = jnp.broadcast_to(length.astype(jnp.float32) - PAGE * place, (128, 128))
    ones = jnp.ones((8, 128, 128), jnp.bfloat16)
    for chunk in range(4, 8):
        kvx[2, chunk] = ones

    def prepare_queries(i):
        for head in range(GROUP):
            block = q_raw[i, :, head * HD:(head + 1) * HD].astype(jnp.float32) * SCALE
            high = block.astype(jnp.bfloat16)
            low = (block - high.astype(jnp.float32)).astype(jnp.bfloat16)
            q_two[i, head * TOK:(head + 1) * TOK, 0:HD] = high
            q_two[i, head * TOK:(head + 1) * TOK, HD:2 * HD] = low

    def prepare_prefix(chunk):
        seen = kvx[0, 4, xc, 0:1, :].astype(jnp.float32)
        row = lax.broadcasted_iota(jnp.int32, (PAGE, 128), 0).astype(jnp.float32)

        def one_block(b, carry):
            for p in range(4):
                limit = limits[pl.ds(chunk * 32 + b * 4 + p, 1), :]
                valid = row < limit
                source = pl.ds(pl.multiple_of(lax.rem(b, 4) * 128 + p * PAGE, PAGE), PAGE)
                key = raw[0, chunk, b // 4, source, :].astype(jnp.float32)
                value = raw[1, chunk, b // 4, source, :].astype(jnp.float32)
                rows = pl.ds(p * PAGE, PAGE)
                kvx[0, chunk, b, rows, :] = jnp.where(valid, key, seen).astype(jnp.bfloat16)
                kvx[1, chunk, b, rows, :] = jnp.where(valid, value, 0.0).astype(jnp.bfloat16)
                kvx[2, chunk, b, rows, :] = jnp.where(valid, 1.0, 0.0).astype(jnp.bfloat16)
            return carry

        lax.fori_loop(0, 8, one_block, 0)

    def attend(i, chunk, count, first=False, diagonal=False):
        width = count * CHUNK

        def scores(r):
            key = kvx[0, pl.ds(chunk, count)].reshape(width, HD)
            two = jnp.concatenate([key, key], axis=1)
            return lax.dot_general(
                q_two[i, r:r + BLOCK, :], two, (((1,), (1,)), ((), ())),
                preferred_element_type=jnp.float32,
            )

        def absorb(r, s):
            if diagonal:
                token = lax.broadcasted_iota(jnp.int32, (BLOCK, CHUNK), 0) % TOK
                key_at = lax.broadcasted_iota(jnp.int32, (BLOCK, CHUNK), 1)
                cut = jnp.where(key_at - token <= xc * TOK, s[:, width - CHUNK:], NEG)
                s = cut if count == 1 else jnp.concatenate([s[:, :width - CHUNK], cut], axis=1)
            rows = slice(r, r + BLOCK)
            value = jnp.concatenate(
                [kvx[1, pl.ds(chunk, count)].reshape(width, HD), kvx[2, pl.ds(chunk, count)].reshape(width, HD)],
                axis=1,
            )
            highest = jnp.max(s, axis=1, keepdims=True)
            if not first:
                before = top[i, rows, :][:, :1]
                highest = jnp.maximum(before, highest)
            weights = jnp.exp2(s - highest).astype(jnp.bfloat16)
            top[i, rows, :] = jnp.broadcast_to(highest, (BLOCK, 128))
            added = jnp.dot(weights, value, preferred_element_type=jnp.float32)
            if first:
                acc[i, rows, :] = added
            else:
                acc[i, rows, :] = acc[i, rows, :] * jnp.exp2(before - highest) + added

        waiting = None
        for r in range(0, ROWS, BLOCK):
            s = scores(r)
            if waiting is not None:
                absorb(*waiting)
            waiting = (r, s)
        absorb(*waiting)

    sib_c = 1 - c
    del sib_c
    pre = lambda rel_x: raw.at[:, rel_x, c]
    low, high = pl.ds(0, 256), pl.ds(256, 256)
    xl, xr, xf = lax.rem(x + 3, 4), lax.rem(x + 1, 4), lax.rem(x + 2, 4)
    suf = lambda xs, part=pl.ds(4, 4): kvx.at[pl.ds(0, 2), part, xs * 2 + c]
    part_a, part_b = pl.ds(4, 2), pl.ds(6, 2)
    pre_plan = {
        "own_s": (pre(0), pre(0), 0, sibling),
        "own_r": (pre(0), pre(1), 1, right),
        "own_l": (pre(0), pre(2), 2, left),
        "far_r": (raw.at[:, 1, c, low], raw.at[:, 3, c, low], 3, right),
        "far_l": (raw.at[:, 2, c, high], raw.at[:, 3, c, high], 4, left),
        "left_s": (pre(1), pre(1), 5, sibling),
        "right_s": (pre(2), pre(2), 6, sibling),
        "fara_s": (raw.at[:, 3, c, low], raw.at[:, 3, c, low], 7, sibling),
        "farb_s": (raw.at[:, 3, c, high], raw.at[:, 3, c, high], 8, sibling),
    }
    suf_plan = {
        "own_s": (suf(x), suf(x), 0, sibling),
        "own_r": (suf(x), suf(x), 1, right),
        "own_l": (suf(x), suf(x), 2, left),
        "far_r": (suf(xl, part_a), suf(xl, part_a), 3, right),
        "far_l": (suf(xr, part_b), suf(xr, part_b), 4, left),
        "left_s": (suf(xl), suf(xl), 5, sibling),
        "right_s": (suf(xr), suf(xr), 6, sibling),
        "fara_s": (suf(xf, part_a), suf(xf, part_a), 7, sibling),
        "farb_s": (suf(xf, part_b), suf(xf, part_b), 8, sibling),
    }

    def pre_copy(name):
        src, dst, number, device = pre_plan[name]
        return remote(src, dst, pre_send.at[number], pre_recv.at[number], device)

    def suf_copy(name):
        src, dst, number, device = suf_plan[name]
        return remote(src, dst, suf_send.at[number], suf_recv.at[number], device)

    own_q.wait()
    prepare_queries(z)
    own_slot = raw.at[:, 0, c]
    pltpu.make_async_copy(own_slot, own_slot, pg_recv).wait()
    for name in ("own_r", "own_l", "own_s"):
        pre_copy(name).start()
    own_new = kvx.at[pl.ds(0, 2), pl.ds(4, 4), xc]
    pltpu.make_async_copy(own_new, own_new, fr_recv).wait()
    for name in ("own_r", "own_l", "own_s"):
        suf_copy(name).start()
    pre_copy("own_s").wait_recv()
    prepare_prefix(0)

    def wait_queries(k, i):
        pltpu.make_async_copy(q_raw.at[i], q_raw.at[i], q_recv.at[k]).wait()
        prepare_queries(i)

    def order(k):
        return lax.rem(z + jnp.where(k < 2, k, 5 - k), 4)

    def phase_a(k, carry):
        i = order(k)

        @pl.when(k > 0)
        def _():
            wait_queries(k, i)

        attend(i, 0, 1, first=True)

        @pl.when(k == 2)
        def _():
            pre_copy("own_r").wait_recv()
            pre_copy("far_r").start()
            pre_copy("left_s").start()
            pre_copy("own_l").wait_recv()
            pre_copy("far_l").start()
            pre_copy("right_s").start()

        return carry

    lax.fori_loop(0, 4, phase_a, 0)
    for copy in written_copies:
        copy.start()
    own_written.start()
    pre_copy("left_s").wait_recv()
    pre_copy("right_s").wait_recv()
    prepare_prefix(1)
    prepare_prefix(2)

    def phase_b(k, carry):
        attend(order(k), 1, 2)

        @pl.when(k == 0)
        def _():
            pre_copy("far_r").wait_recv()
            pre_copy("fara_s").start()
            pre_copy("far_l").wait_recv()
            pre_copy("farb_s").start()

        @pl.when(k == 1)
        def _():
            suf_copy("own_r").wait_recv()
            suf_copy("far_r").start()
            suf_copy("left_s").start()
            suf_copy("own_l").wait_recv()
            suf_copy("far_l").start()
            suf_copy("right_s").start()

        @pl.when(k == 3)
        def _():
            suf_copy("far_r").wait_recv()
            suf_copy("fara_s").start()
            suf_copy("far_l").wait_recv()
            suf_copy("farb_s").start()

        return carry

    lax.fori_loop(0, 4, phase_b, 0)
    for name in ("fara_s", "farb_s"):
        pre_copy(name).wait_recv()
    prepare_prefix(3)
    for name in ("own_s", "left_s", "right_s", "fara_s", "farb_s"):
        suf_copy(name).wait_recv()

    def out_copy(i):
        return remote(
            o_buf.at[i], attended.at[0, :, lanes(z * ROWS, ROWS)], o_send.at[i], o_recv, (y, i * 8 + xc)
        )

    def own_out():
        return pltpu.make_async_copy(o_buf.at[z], attended.at[0, :, lanes(z * ROWS, ROWS)], o_recv)

    def phase_c(k, carry):
        i = lax.rem(z + jnp.where(k == 0, 2, jnp.where(k == 1, 1, jnp.where(k == 2, 3, 0))), 4)

        @pl.when(i == 0)
        def _():
            attend(i, 3, 2, diagonal=True)

        @pl.when(i > 0)
        def _():
            lax.fori_loop(0, jnp.where(i == 3, 2, 1), lambda t, u: (attend(i, 3 + 2 * t, 2), u)[1], 0)

        @pl.when(i == 2)
        def _():
            attend(i, 5, 2, diagonal=True)

        @pl.when(lax.rem(i, 2) == 1)
        def _():
            attend(i, 4 + i, 1, diagonal=True)

        for head in range(GROUP):
            rows = slice(head * TOK, (head + 1) * TOK)
            o_buf[i, :, head * HD:(head + 1) * HD] = (
                acc[i, rows, 0:HD] / acc[i, rows, HD:2 * HD]
            ).astype(jnp.bfloat16)

        @pl.when(k < 3)
        def _():
            out_copy(i).start()

        @pl.when(k == 3)
        def _():
            own_out().start()

        return carry

    lax.fori_loop(0, 4, phase_c, 0)

    for copy in page_copies + fresh_copies + list(q_copies.values()) + written_copies:
        copy.wait_send()
    for name in pre_plan:
        pre_copy(name).wait_send()
        suf_copy(name).wait_send()
    pltpu.make_async_copy(written, written, np_recv).wait()
    for dz in (1, 3, 2):
        out_copy(lax.rem(z + dz, 4)).wait_send()
    pltpu.make_async_copy(attended, attended, o_recv).wait()


def per_device(queries, fresh_cache, page_store, page_table, prefix_lengths):
    anywhere = pl.BlockSpec(memory_space=pl.ANY)
    bf16, f32 = jnp.bfloat16, jnp.float32
    dma = pltpu.SemaphoreType.DMA
    return pl.pallas_call(
        kernel,
        out_shape=(
            jax.ShapeDtypeStruct((1, TOK, H * HD), bf16),
            jax.ShapeDtypeStruct((1, 4, 1, PAGE, 2 * KVH * HD), bf16),
        ),
        in_specs=[
            anywhere, anywhere, anywhere,
            pl.BlockSpec(memory_space=pltpu.VMEM),
            pl.BlockSpec(memory_space=pltpu.SMEM),
        ],
        out_specs=(anywhere, anywhere),
        scratch_shapes=[
            pltpu.VMEM((3, 8, 8, 128, HD), bf16),
            pltpu.VMEM((2, 4, 2, 512, HD), bf16),
            pltpu.VMEM((4, TOK, ROWS), bf16),
            pltpu.VMEM((4, ROWS, 2 * HD), bf16),
            pltpu.VMEM((4, ROWS, 2 * HD), f32),
            pltpu.VMEM((4, ROWS, 128), f32),
            pltpu.VMEM((4, TOK, ROWS), bf16),
            pltpu.VMEM((128, 128), f32),
            dma((30,)), dma, dma((6,)), dma, dma((3,)), dma((4,)), dma((4,)), dma,
            dma((3,)), dma, dma((9,)), dma((9,)), dma((9,)), dma((9,)),
        ],
        compiler_params=pltpu.CompilerParams(
            collective_id=0, has_side_effects=True, vmem_limit_bytes=56 * 2**20
        ),
        cost_estimate=pl.CostEstimate(flops=2 * 2 * 4096 * 6656 * 128, bytes_accessed=4 * 2**20, transcendentals=4096 * 6656),
    )(queries, fresh_cache, page_store, page_table, prefix_lengths)


def solution(mesh):
    placed = (P("req", "blk", None), P("req", "blk", None), P(("req", "blk"), None, None), P(), P())
    return jax.shard_map(
        per_device,
        mesh=mesh,
        in_specs=placed,
        out_specs=(P("req", "blk", None), P("req", None, "blk", None, None)),
        check_vma=False,
    )
```

profile of v0, /device:TPU:1, one launch (start us, length us, event | category | flops | bytes accessed | tf_op | source)
XLA Modules:
  0.0 72.4 jit_solution(12420871043057982442)
XLA Ops:
  0.6 68.7 %shard_map.68 = (bf16[1,128,4096]{2,1,0:T(8,128)(2,1)}, bf16[1,4,1,32,1024]{4,3,2,1,0:T(8,128)(2,1)}) custom-call(bf16[1,128,4096]{2,1,0:T(8,128)(2,1)} %queries.1, bf16[1,128,1024]{2,1,0:T(8,128)(2,1)} %fresh.1, bf16[4,32,1024]{2,1,0:T(8,128)(2,1)} %pages.1, s32[4,128]{1,0:T(4,128)} %table.1, s32[4]{0:T(128)} %lengths.1), custom_call_target="tpu_custom_call" | custom-call | flops 13958643712 | bytes 4194304 | tf_op jit(solution)/shard_map/pallas_call | solution.py:390
  69.3 0.0 copy-start
  69.3 2.3 %copy.9 = bf16[1,128,4096]{2,1,0:T(8,128)(2,1)} copy(bf16[1,128,4096]{2,1,0:T(8,128)(2,1)} %get-tuple-element.4) | data formatting | bytes 2097152
  71.7 0.0 copy-done
  71.7 0.7 copy.10
Async XLA Ops:
  69.3 2.3 %copy-start = (bf16[1,4,1,32,1024]{4,3,2,1,0:T(8,128)(2,1)S(1)}, bf16[1,4,1,32,1024]{4,3,2,1,0:T(8,128)(2,1)}, u32[]{:S(2)}) copy-start(bf16[1,4,1,32,1024]{4,3,2,1,0:T(8,128)(2,1)} %get-tuple-element.5) | copy-start | bytes 786436
where the time goes:
time: 72.5 us; the launch traced here: 72.4 us
  Pallas kernels  68.7 us (95%)
  local copies, waits for them, and re-layouts  3.04 us (4%)
    pallas_call x1, Pallas kernels, per_device(): pl.pallas_call(kernel, out_shape=(jax.ShapeDtypeStruct((1, TOK, H * HD),...  68.7 us
    unnamed x4, local copies, waits for them, and re-layouts  3.04 us

commit v1 on v0

--- a/solution.py
+++ b/solution.py
@@ -25,7 +25,7 @@
 def kernel(
     queries, fresh, pages, table, lengths, attended, written,
     kvx, raw, q_raw, q_two, acc, top, o_buf, limits,
-    pg_send, pg_recv, fr_send, fr_recv, q_send, q_recv, o_send, o_recv,
+    paged, py_send, py_recv, pg_send, pg_recv, fr_send, fr_recv, q_send, q_recv, o_send, o_recv,
     np_send, np_recv, pre_send, pre_recv, suf_send, suf_recv,
 ):
     y = lax.axis_index("req")
@@ -44,89 +44,62 @@
         )
 
     right, left, sibling = at(0, 0, 1, 0), at(0, 0, 3, 0), at(0, 0, 0, 1)
-    others = [(dy, dz) for dz in (0, 1, 3, 2) for dy in (0, 1, 3, 2) if dy or dz]
-    greeted = [at(dy, dz, 0, 0) for dy, dz in others] + [right, left, sibling]
+    greeted = [at(dy, 0, 0, 0) for dy in (1, 3, 2)] + [at(0, dz, 0, 0) for dz in (1, 3, 2)]
+    greeted += [right, left, sibling]
     barrier = pltpu.get_barrier_semaphore()
     for device in greeted:
         pl.semaphore_signal(barrier, inc=1, device_id=device, device_id_type=MESH)
-    pl.semaphore_wait(barrier, len(greeted))
 
     def lanes(first, size=HD):
         return pl.ds(pl.multiple_of(first, HD), size)
 
-    my_rows = pl.ds(pl.multiple_of((y * 4 + z) * PAGE, PAGE), PAGE)
-    page_copies = []
-    n = 0
-    for dy, dz in others:
-        y2, z2 = lax.rem(y + dy, 4), lax.rem(z + dz, 4)
-        for plane in range(2):
-            page_copies.append(remote(
-                pages.at[y2, :, lanes(plane * 512 + z2 * HD)],
-                raw.at[plane, 0, c, my_rows],
-                pg_send.at[n], pg_recv, at(dy, dz, 0, 0),
-            ))
-            n += 1
-    for copy in page_copies:
-        copy.start()
-    own_pages = [
-        pltpu.make_async_copy(
-            pages.at[y, :, lanes(plane * 512 + z * HD)], raw.at[plane, 0, c, my_rows], pg_recv
-        )
-        for plane in range(2)
-    ]
-    for copy in own_pages:
-        copy.start()
-
-    own_q = pltpu.make_async_copy(queries.at[0, :, lanes(z * ROWS, ROWS)], q_raw.at[z], q_recv.at[0])
-    own_q.start()
+    def page_rows(first):
+        return pl.ds(pl.multiple_of(first * PAGE, PAGE), PAGE)
+
     xc = x * 2 + c
-    fresh_copies = []
-    n = 0
-    for dz in (1, 3, 2):
+    slab = pl.ds(pl.multiple_of(z * TOK, TOK), TOK)
+    page_copies, slab_copies, fresh_copies, written_copies = [], [], [], []
+    for k, dy in enumerate((1, 3, 2)):
+        y2 = lax.rem(y + dy, 4)
+        page_copies.append(remote(
+            pages.at[y2], paged.at[page_rows(y)], py_send.at[k], py_recv, at(dy, 0, 0, 0)
+        ))
+        written_copies.append(remote(
+            fresh.at[0, page_rows(y2)], written.at[0, y, 0], np_send.at[k], np_recv, at(dy, 0, 0, 0)
+        ))
+    own_page = pltpu.make_async_copy(pages.at[y], paged.at[page_rows(y)], py_recv)
+    own_written = pltpu.make_async_copy(fresh.at[0, page_rows(y)], written.at[0, y, 0], np_recv)
+    q_copies = []
+    for k, dz in enumerate((1, 3, 2)):
         z2 = lax.rem(z + dz, 4)
         for plane in range(2):
+            head = lanes(plane * 512 + z2 * HD)
+            slab_copies.append(remote(
+                paged.at[:, head], raw.at[plane, 0, c, slab], pg_send.at[2 * k + plane], pg_recv, at(0, dz, 0, 0)
+            ))
             fresh_copies.append(remote(
-                fresh.at[0, :, lanes(plane * 512 + z2 * HD)],
-                kvx.at[plane, 4 + z, xc],
-                fr_send.at[n], fr_recv, at(0, dz, 0, 0),
+                fresh.at[0, :, head], kvx.at[plane, 4 + z, xc], fr_send.at[2 * k + plane], fr_recv, at(0, dz, 0, 0)
             ))
-            n += 1
-    for copy in fresh_copies:
-        copy.start()
-    own_fresh = [
-        pltpu.make_async_copy(
-            fresh.at[0, :, lanes(plane * 512 + z * HD)], kvx.at[plane, 4 + z, xc], fr_recv
-        )
-        for plane in range(2)
-    ]
-    for copy in own_fresh:
-        copy.start()
-    q_copies = {}
-    for k, dz in enumerate((1, 3, 2)):
-        z2 = lax.rem(z + dz, 4)
         k_there = {1: 2, 3: 1, 2: 3}[dz]
-        q_copies[k] = remote(
+        q_copies.append(remote(
             queries.at[0, :, lanes(z2 * ROWS, ROWS)], q_raw.at[z],
             q_send.at[k], q_recv.at[k_there], at(0, dz, 0, 0),
-        )
-        q_copies[k].start()
-    written_copies = []
-    for k, dy in enumerate((1, 2, 3)):
-        y2 = lax.rem(y + dy, 4)
-        written_copies.append(remote(
-            fresh.at[0, pl.ds(pl.multiple_of(y2 * PAGE, PAGE), PAGE)], written.at[0, y, 0],
-            np_send.at[k], np_recv, at(dy, 0, 0, 0),
         ))
-    own_written = pltpu.make_async_copy(
-        fresh.at[0, pl.ds(pl.multiple_of(y * PAGE, PAGE), PAGE)], written.at[0, y, 0], np_recv
-    )
+    own_slab, own_fresh = [], []
+    for plane in range(2):
+        head = lanes(plane * 512 + z * HD)
+        own_slab.append(pltpu.make_async_copy(paged.at[:, head], raw.at[plane, 0, c, slab], pg_recv))
+        own_fresh.append(pltpu.make_async_copy(fresh.at[0, :, head], kvx.at[plane, 4 + z, xc], fr_recv))
+    own_q = pltpu.make_async_copy(queries.at[0, :, lanes(z * ROWS, ROWS)], q_raw.at[z], q_recv.at[0])
+    for copy in [own_q, own_page] + own_fresh:
+        copy.start()
 
     length = lengths[y]
     j = lax.broadcasted_iota(jnp.int32, (128, 128), 0)
     rel = j // 32
     x_of = lax.rem(x + jnp.where(rel == 0, 0, jnp.where(rel == 1, 3, jnp.where(rel == 2, 1, 2))), 4)
     c_of = (j // 16) % 2
-    y_of, z_of = (j // 4) % 4, j % 4
+    z_of, y_of = (j // 4) % 4, j % 4
     slot = 4 * (y_of * 32 + z_of * 8 + x_of * 2 + c_of) + y
     page = lax.broadcasted_iota(jnp.int32, (128, 128), 1)
     match = jnp.broadcast_to(table[pl.ds(y, 1), :], (128, 128)) == slot
@@ -205,8 +178,6 @@
             waiting = (r, s)
         absorb(*waiting)
 
-    sib_c = 1 - c
-    del sib_c
     pre = lambda rel_x: raw.at[:, rel_x, c]
     low, high = pl.ds(0, 256), pl.ds(256, 256)
     xl, xr, xf = lax.rem(x + 3, 4), lax.rem(x + 1, 4), lax.rem(x + 2, 4)
@@ -243,23 +214,33 @@
         src, dst, number, device = suf_plan[name]
         return remote(src, dst, suf_send.at[number], suf_recv.at[number], device)
 
+    def wait_queries(k, i):
+        pltpu.make_async_copy(q_raw.at[i], q_raw.at[i], q_recv.at[k]).wait()
+        prepare_queries(i)
+
     own_q.wait()
     prepare_queries(z)
+    pl.semaphore_wait(barrier, len(greeted))
+    for copy in page_copies + q_copies[:2]:
+        copy.start()
+    pltpu.make_async_copy(paged, paged, py_recv).wait()
+    for copy in slab_copies + own_slab:
+        copy.start()
     own_slot = raw.at[:, 0, c]
     pltpu.make_async_copy(own_slot, own_slot, pg_recv).wait()
     for name in ("own_r", "own_l", "own_s"):
         pre_copy(name).start()
+    for copy in fresh_copies:
+        copy.start()
     own_new = kvx.at[pl.ds(0, 2), pl.ds(4, 4), xc]
     pltpu.make_async_copy(own_new, own_new, fr_recv).wait()
     for name in ("own_r", "own_l", "own_s"):
         suf_copy(name).start()
+    for copy in [q_copies[2], own_written] + written_copies:
+        copy.start()
     pre_copy("own_s").wait_recv()
     prepare_prefix(0)
 
-    def wait_queries(k, i):
-        pltpu.make_async_copy(q_raw.at[i], q_raw.at[i], q_recv.at[k]).wait()
-        prepare_queries(i)
-
     def order(k):
         return lax.rem(z + jnp.where(k < 2, k, 5 - k), 4)
 
@@ -271,29 +252,24 @@
             wait_queries(k, i)
 
         attend(i, 0, 1, first=True)
-
-        @pl.when(k == 2)
-        def _():
-            pre_copy("own_r").wait_recv()
-            pre_copy("far_r").start()
-            pre_copy("left_s").start()
-            pre_copy("own_l").wait_recv()
-            pre_copy("far_l").start()
-            pre_copy("right_s").start()
-
         return carry
 
-    lax.fori_loop(0, 4, phase_a, 0)
-    for copy in written_copies:
-        copy.start()
-    own_written.start()
+    lax.fori_loop(0, 3, phase_a, 0)
+    pre_copy("own_r").wait_recv()
+    pre_copy("far_r").start()
+    pre_copy("left_s").start()
+    pre_copy("own_l").wait_recv()
+    pre_copy("far_l").start()
+    pre_copy("right_s").start()
     pre_copy("left_s").wait_recv()
+    prepare_prefix(1)
     pre_copy("right_s").wait_recv()
-    prepare_prefix(1)
     prepare_prefix(2)
 
     def phase_b(k, carry):
-        attend(order(k), 1, 2)
+        @pl.when(k < 3)
+        def _():
+            attend(lax.rem(z + jnp.where(k == 0, 1, jnp.where(k == 1, 3, 0)), 4), 1, 2)
 
         @pl.when(k == 0)
         def _():
@@ -313,6 +289,9 @@
 
         @pl.when(k == 3)
         def _():
+            i = lax.rem(z + 2, 4)
+            wait_queries(3, i)
+            attend(i, 0, 3, first=True)
             suf_copy("far_r").wait_recv()
             suf_copy("fara_s").start()
             suf_copy("far_l").wait_recv()
@@ -342,17 +321,17 @@
         def _():
             attend(i, 3, 2, diagonal=True)
 
-        @pl.when(i > 0)
-        def _():
-            lax.fori_loop(0, jnp.where(i == 3, 2, 1), lambda t, u: (attend(i, 3 + 2 * t, 2), u)[1], 0)
+        @pl.when(i == 3)
+        def _():
+            attend(i, 3, 2)
+
+        @pl.when(lax.rem(i, 2) == 1)
+        def _():
+            attend(i, 2 + i, 3, diagonal=True)
 
         @pl.when(i == 2)
         def _():
-            attend(i, 5, 2, diagonal=True)
-
-        @pl.when(lax.rem(i, 2) == 1)
-        def _():
-            attend(i, 4 + i, 1, diagonal=True)
+            attend(i, 3, 4, diagonal=True)
 
         for head in range(GROUP):
             rows = slice(head * TOK, (head + 1) * TOK)
@@ -372,7 +351,7 @@
 
     lax.fori_loop(0, 4, phase_c, 0)
 
-    for copy in page_copies + fresh_copies + list(q_copies.values()) + written_copies:
+    for copy in page_copies + slab_copies + fresh_copies + q_copies + written_copies:
         copy.wait_send()
     for name in pre_plan:
         pre_copy(name).wait_send()
@@ -383,16 +362,30 @@
     pltpu.make_async_copy(attended, attended, o_recv).wait()
 
 
+def hand_over(attended_in, written_in, attended, written, sems):
+    rows = [pl.ds(32 * k, 32) for k in range(4)]
+    copies = [
+        pltpu.make_async_copy(attended_in.at[0, part], attended.at[0, part], sems.at[k])
+        for k, part in enumerate(rows)
+    ]
+    copies.append(pltpu.make_async_copy(written_in, written, sems.at[4]))
+    for copy in copies:
+        copy.start()
+    for copy in copies:
+        copy.wait()
+
+
 def per_device(queries, fresh_cache, page_store, page_table, prefix_lengths):
     anywhere = pl.BlockSpec(memory_space=pl.ANY)
     bf16, f32 = jnp.bfloat16, jnp.float32
     dma = pltpu.SemaphoreType.DMA
-    return pl.pallas_call(
+    outs_shape = (
+        jax.ShapeDtypeStruct((1, TOK, H * HD), bf16),
+        jax.ShapeDtypeStruct((1, 4, 1, PAGE, 2 * KVH * HD), bf16),
+    )
+    outs = pl.pallas_call(
         kernel,
-        out_shape=(
-            jax.ShapeDtypeStruct((1, TOK, H * HD), bf16),
-            jax.ShapeDtypeStruct((1, 4, 1, PAGE, 2 * KVH * HD), bf16),
-        ),
+        out_shape=outs_shape,
         in_specs=[
             anywhere, anywhere, anywhere,
             pl.BlockSpec(memory_space=pltpu.VMEM),
@@ -408,7 +401,8 @@
             pltpu.VMEM((4, ROWS, 128), f32),
             pltpu.VMEM((4, TOK, ROWS), bf16),
             pltpu.VMEM((128, 128), f32),
-            dma((30,)), dma, dma((6,)), dma, dma((3,)), dma((4,)), dma((4,)), dma,
+            pltpu.VMEM((4 * PAGE, 2 * KVH * HD), bf16),
+            dma((3,)), dma, dma((6,)), dma, dma((6,)), dma, dma((3,)), dma((4,)), dma((4,)), dma,
             dma((3,)), dma, dma((9,)), dma((9,)), dma((9,)), dma((9,)),
         ],
         compiler_params=pltpu.CompilerParams(
@@ -416,6 +410,13 @@
         ),
         cost_estimate=pl.CostEstimate(flops=2 * 2 * 4096 * 6656 * 128, bytes_accessed=4 * 2**20, transcendentals=4096 * 6656),
     )(queries, fresh_cache, page_store, page_table, prefix_lengths)
+    return pl.pallas_call(
+        hand_over,
+        out_shape=outs_shape,
+        in_specs=[anywhere, anywhere],
+        out_specs=(anywhere, anywhere),
+        scratch_shapes=[dma((5,))],
+    )(*outs)
 
 
 def solution(mesh):

time: 72.5 us -> 111 us (1.53)
  Pallas kernels: 68.7 us -> 110 us
  local copies, waits for them, and re-layouts: 3.04 us -> 0 us
    pallas_call x1 -> x2, Pallas kernels: 68.7 us -> 110 us  [the longest x1 69.3 us: per_device(): pl.pallas_call(kernel, out_shape=outs_shape, in_specs=[anywhere, anywhere...]
    unnamed x4 -> x0, local copies, waits for them, and re-layouts: 3.04 us -> none
where the time goes in v1:
time: 111 us
  Pallas kernels  110 us (99%)
    pallas_call x1, Pallas kernels, per_device(): pl.pallas_call(kernel, out_shape=outs_shape, in_specs=[anywhere, anywhere...  69.3 us
    pallas_call x1, Pallas kernels, per_device(): pl.pallas_call(hand_over, out_shape=outs_shape, in_specs=[anywhere, anywh...  40.9 us

profile of v1, /device:TPU:1, one launch (start us, length us, event | category | flops | bytes accessed | tf_op | source)
XLA Modules:
  0.0 111.0 jit_solution(11084816139992203483)
XLA Ops:
  0.6 69.3 %shard_map.68 = (bf16[1,128,4096]{2,1,0:T(8,128)(2,1)}, bf16[1,4,1,32,1024]{4,3,2,1,0:T(8,128)(2,1)}) custom-call(bf16[1,128,4096]{2,1,0:T(8,128)(2,1)} %queries.1, bf16[1,128,1024]{2,1,0:T(8,128)(2,1)} %fresh.1, bf16[4,32,1024]{2,1,0:T(8,128)(2,1)} %pages.1, s32[4,128]{1,0:T(4,128)} %table.1, s32[4]{0:T(128)} %lengths.1), custom_call_target="tpu_custom_call" | custom-call | flops 13958643712 | bytes 4194304 | tf_op jit(solution)/shard_map/pallas_call | solution.py:386
  69.9 40.9 %shard_map.69 = (bf16[1,128,4096]{2,1,0:T(8,128)(2,1)}, bf16[1,4,1,32,1024]{4,3,2,1,0:T(8,128)(2,1)}) custom-call(bf16[1,128,4096]{2,1,0:T(8,128)(2,1)} %get-tuple-element.4.attended_in, bf16[1,4,1,32,1024]{4,3,2,1,0:T(8,128)(2,1)} %get-tuple-element.5.written_in), custom_call_target="tpu_custom_call" | custom-call | tf_op jit(solution)/shard_map/pallas_call | solution.py:413

commit v2 on v1

--- a/solution.py
+++ b/solution.py
@@ -16,6 +16,7 @@
 PAGE = 32
 CHUNK = 1024
 ROWS = GROUP * TOK
+HALF = ROWS // 2
 NEG = -1e30
 SCALE = math.log2(math.e) / math.sqrt(HD)
 MESH = pl.DeviceIdType.MESH
@@ -25,7 +26,7 @@
 def kernel(
     queries, fresh, pages, table, lengths, attended, written,
     kvx, raw, q_raw, q_two, acc, top, o_buf, limits,
-    paged, py_send, py_recv, pg_send, pg_recv, fr_send, fr_recv, q_send, q_recv, o_send, o_recv,
+    paged, seen_key, se_send, se_recv, py_send, py_recv, pg_send, pg_recv, fr_send, fr_recv, q_send, q_recv, o_send, o_recv,
     np_send, np_recv, pre_send, pre_recv, suf_send, suf_recv,
 ):
     y = lax.axis_index("req")
@@ -69,7 +70,7 @@
         ))
     own_page = pltpu.make_async_copy(pages.at[y], paged.at[page_rows(y)], py_recv)
     own_written = pltpu.make_async_copy(fresh.at[0, page_rows(y)], written.at[0, y, 0], np_recv)
-    q_copies = []
+    q_copies, seen_copies = [], []
     for k, dz in enumerate((1, 3, 2)):
         z2 = lax.rem(z + dz, 4)
         for plane in range(2):
@@ -80,11 +81,21 @@
             fresh_copies.append(remote(
                 fresh.at[0, :, head], kvx.at[plane, 4 + z, xc], fr_send.at[2 * k + plane], fr_recv, at(0, dz, 0, 0)
             ))
-        k_there = {1: 2, 3: 1, 2: 3}[dz]
-        q_copies.append(remote(
-            queries.at[0, :, lanes(z2 * ROWS, ROWS)], q_raw.at[z],
-            q_send.at[k], q_recv.at[k_there], at(0, dz, 0, 0),
+        if dz == 2:
+            q_far = remote(
+                queries.at[0, :, lanes(z2 * ROWS, ROWS)], q_raw.at[z], q_send.at[4], q_recv.at[5], at(0, dz, 0, 0)
+            )
+        else:
+            for half in range(2):
+                q_copies.append(remote(
+                    queries.at[0, :, lanes(z2 * ROWS + half * HALF, HALF)],
+                    q_raw.at[z, :, half * HALF:(half + 1) * HALF],
+                    q_send.at[2 * k + half], q_recv.at[{1: 3, 3: 1}[dz] + half], at(0, dz, 0, 0),
+                ))
+        seen_copies.append(remote(
+            fresh.at[0, 0:16, lanes(z2 * HD)], seen_key, se_send.at[k], se_recv, at(0, dz, 0, 0)
         ))
+    own_seen = pltpu.make_async_copy(fresh.at[0, 0:16, lanes(z * HD)], seen_key, se_recv)
     own_slab, own_fresh = [], []
     for plane in range(2):
         head = lanes(plane * 512 + z * HD)
@@ -109,8 +120,8 @@
     for chunk in range(4, 8):
         kvx[2, chunk] = ones
 
-    def prepare_queries(i):
-        for head in range(GROUP):
+    def prepare_queries(i, first=0, last=GROUP):
+        for head in range(first, last):
             block = q_raw[i, :, head * HD:(head + 1) * HD].astype(jnp.float32) * SCALE
             high = block.astype(jnp.bfloat16)
             low = (block - high.astype(jnp.float32)).astype(jnp.bfloat16)
@@ -118,7 +129,7 @@
             q_two[i, head * TOK:(head + 1) * TOK, HD:2 * HD] = low
 
     def prepare_prefix(chunk):
-        seen = kvx[0, 4, xc, 0:1, :].astype(jnp.float32)
+        seen = seen_key[...].astype(jnp.float32)[0:1, :]
         row = lax.broadcasted_iota(jnp.int32, (PAGE, 128), 0).astype(jnp.float32)
 
         def one_block(b, carry):
@@ -136,24 +147,24 @@
 
         lax.fori_loop(0, 8, one_block, 0)
 
-    def attend(i, chunk, count, first=False, diagonal=False):
+    def attend(i, chunk, count, first=False, diagonal=False, blocks=None):
+        blocks = blocks or [(i, slice(r, r + BLOCK)) for r in range(0, ROWS, BLOCK)]
         width = count * CHUNK
 
-        def scores(r):
+        def scores(i, rows):
             key = kvx[0, pl.ds(chunk, count)].reshape(width, HD)
             two = jnp.concatenate([key, key], axis=1)
             return lax.dot_general(
-                q_two[i, r:r + BLOCK, :], two, (((1,), (1,)), ((), ())),
+                q_two[i, rows, :], two, (((1,), (1,)), ((), ())),
                 preferred_element_type=jnp.float32,
             )
 
-        def absorb(r, s):
+        def absorb(i, rows, s):
             if diagonal:
                 token = lax.broadcasted_iota(jnp.int32, (BLOCK, CHUNK), 0) % TOK
                 key_at = lax.broadcasted_iota(jnp.int32, (BLOCK, CHUNK), 1)
                 cut = jnp.where(key_at - token <= xc * TOK, s[:, width - CHUNK:], NEG)
                 s = cut if count == 1 else jnp.concatenate([s[:, :width - CHUNK], cut], axis=1)
-            rows = slice(r, r + BLOCK)
             value = jnp.concatenate(
                 [kvx[1, pl.ds(chunk, count)].reshape(width, HD), kvx[2, pl.ds(chunk, count)].reshape(width, HD)],
                 axis=1,
@@ -171,11 +182,11 @@
                 acc[i, rows, :] = acc[i, rows, :] * jnp.exp2(before - highest) + added
 
         waiting = None
-        for r in range(0, ROWS, BLOCK):
-            s = scores(r)
+        for i, rows in blocks:
+            s = scores(i, rows)
             if waiting is not None:
                 absorb(*waiting)
-            waiting = (r, s)
+            waiting = (i, rows, s)
         absorb(*waiting)
 
     pre = lambda rel_x: raw.at[:, rel_x, c]
@@ -214,14 +225,21 @@
         src, dst, number, device = suf_plan[name]
         return remote(src, dst, suf_send.at[number], suf_recv.at[number], device)
 
-    def wait_queries(k, i):
-        pltpu.make_async_copy(q_raw.at[i], q_raw.at[i], q_recv.at[k]).wait()
-        prepare_queries(i)
+    def wait_queries(i, number, half=None):
+        part = q_raw.at[i] if half is None else q_raw.at[i, :, half * HALF:(half + 1) * HALF]
+        pltpu.make_async_copy(part, part, q_recv.at[number]).wait()
+        prepare_queries(i, *((0, GROUP) if half is None else (half * GROUP // 2, (half + 1) * GROUP // 2)))
 
     own_q.wait()
     prepare_queries(z)
     pl.semaphore_wait(barrier, len(greeted))
-    for copy in page_copies + q_copies[:2]:
+
+    @pl.when(z == 0)
+    def _():
+        for copy in seen_copies + [own_seen]:
+            copy.start()
+
+    for copy in page_copies + q_copies[0::2]:
         copy.start()
     pltpu.make_async_copy(paged, paged, py_recv).wait()
     for copy in slab_copies + own_slab:
@@ -230,28 +248,26 @@
     pltpu.make_async_copy(own_slot, own_slot, pg_recv).wait()
     for name in ("own_r", "own_l", "own_s"):
         pre_copy(name).start()
-    for copy in fresh_copies:
-        copy.start()
-    own_new = kvx.at[pl.ds(0, 2), pl.ds(4, 4), xc]
-    pltpu.make_async_copy(own_new, own_new, fr_recv).wait()
-    for name in ("own_r", "own_l", "own_s"):
-        suf_copy(name).start()
-    for copy in [q_copies[2], own_written] + written_copies:
-        copy.start()
+    for copy in q_copies[1::2] + fresh_copies:
+        copy.start()
+    pltpu.make_async_copy(seen_key, seen_key, se_recv).wait()
     pre_copy("own_s").wait_recv()
     prepare_prefix(0)
-
-    def order(k):
-        return lax.rem(z + jnp.where(k < 2, k, 5 - k), 4)
+    up, down = lax.rem(z + 1, 4), lax.rem(z + 3, 4)
 
     def phase_a(k, carry):
-        i = order(k)
-
-        @pl.when(k > 0)
-        def _():
-            wait_queries(k, i)
-
-        attend(i, 0, 1, first=True)
+        for half in range(2):
+            @pl.when(k == 1 + half)
+            def _():
+                wait_queries(up, 1 + half, half)
+                wait_queries(down, 3 + half, half)
+
+        blocks = []
+        for b in range(4):
+            i = jnp.where(k == 0, z, up if b < 2 else down)
+            r = jnp.where(k == 0, b * BLOCK, (b % 2) * BLOCK + (k - 1) * HALF)
+            blocks.append((i, pl.ds(pl.multiple_of(r, BLOCK), BLOCK)))
+        attend(None, 0, 1, first=True, blocks=blocks)
         return carry
 
     lax.fori_loop(0, 3, phase_a, 0)
@@ -261,15 +277,21 @@
     pre_copy("own_l").wait_recv()
     pre_copy("far_l").start()
     pre_copy("right_s").start()
+    own_new = kvx.at[pl.ds(0, 2), pl.ds(4, 4), xc]
+    pltpu.make_async_copy(own_new, own_new, fr_recv).wait()
+    for name in ("own_r", "own_l", "own_s"):
+        suf_copy(name).start()
+    for copy in [q_far, own_written] + written_copies:
+        copy.start()
     pre_copy("left_s").wait_recv()
     prepare_prefix(1)
     pre_copy("right_s").wait_recv()
     prepare_prefix(2)
 
     def phase_b(k, carry):
-        @pl.when(k < 3)
-        def _():
-            attend(lax.rem(z + jnp.where(k == 0, 1, jnp.where(k == 1, 3, 0)), 4), 1, 2)
+        @pl.when(k < 2)
+        def _():
+            attend(jnp.where(k == 0, up, down), 1, 2)
 
         @pl.when(k == 0)
         def _():
@@ -287,10 +309,10 @@
             suf_copy("far_l").start()
             suf_copy("right_s").start()
 
-        @pl.when(k == 3)
+        @pl.when(k == 2)
         def _():
             i = lax.rem(z + 2, 4)
-            wait_queries(3, i)
+            wait_queries(i, 5)
             attend(i, 0, 3, first=True)
             suf_copy("far_r").wait_recv()
             suf_copy("fara_s").start()
@@ -299,7 +321,7 @@
 
         return carry
 
-    lax.fori_loop(0, 4, phase_b, 0)
+    lax.fori_loop(0, 3, phase_b, 0)
     for name in ("fara_s", "farb_s"):
         pre_copy(name).wait_recv()
     prepare_prefix(3)
@@ -321,9 +343,9 @@
         def _():
             attend(i, 3, 2, diagonal=True)
 
-        @pl.when(i == 3)
-        def _():
-            attend(i, 3, 2)
+        lax.fori_loop(
+            jnp.where(k == 3, 0, 1), jnp.where(i == 3, 2, 1), lambda u, done: (attend(i, 1 + 2 * u, 2), done)[1], 0
+        )
 
         @pl.when(lax.rem(i, 2) == 1)
         def _():
@@ -351,8 +373,14 @@
 
     lax.fori_loop(0, 4, phase_c, 0)
 
-    for copy in page_copies + slab_copies + fresh_copies + q_copies + written_copies:
+    for copy in page_copies + slab_copies + fresh_copies + q_copies + [q_far] + written_copies:
         copy.wait_send()
+
+    @pl.when(z == 0)
+    def _():
+        for copy in seen_copies:
+            copy.wait_send()
+
     for name in pre_plan:
         pre_copy(name).wait_send()
         suf_copy(name).wait_send()
@@ -362,16 +390,17 @@
     pltpu.make_async_copy(attended, attended, o_recv).wait()
 
 
-def hand_over(attended_in, written_in, attended, written, sems):
-    rows = [pl.ds(32 * k, 32) for k in range(4)]
-    copies = [
-        pltpu.make_async_copy(attended_in.at[0, part], attended.at[0, part], sems.at[k])
-        for k, part in enumerate(rows)
-    ]
-    copies.append(pltpu.make_async_copy(written_in, written, sems.at[4]))
-    for copy in copies:
-        copy.start()
-    for copy in copies:
+def hand_over(attended_in, written_in, attended, written, rows_buf, pages_buf, sems):
+    parts = [(attended_in.at[0, part], rows_buf.at[part], attended.at[0, part]) for part in (pl.ds(32 * k, 32) for k in range(4))]
+    parts.append((written_in, pages_buf, written))
+    arrive = [pltpu.make_async_copy(a, b, sems.at[0, k]) for k, (a, b, _) in enumerate(parts)]
+    leave = [pltpu.make_async_copy(b, a, sems.at[1, k]) for k, (_, b, a) in enumerate(parts)]
+    for copy in arrive:
+        copy.start()
+    for one, other in zip(arrive, leave):
+        one.wait()
+        other.start()
+    for copy in leave:
         copy.wait()
 
 
@@ -402,7 +431,8 @@
             pltpu.VMEM((4, TOK, ROWS), bf16),
             pltpu.VMEM((128, 128), f32),
             pltpu.VMEM((4 * PAGE, 2 * KVH * HD), bf16),
-            dma((3,)), dma, dma((6,)), dma, dma((6,)), dma, dma((3,)), dma((4,)), dma((4,)), dma,
+            pltpu.VMEM((16, HD), bf16),
+            dma((3,)), dma, dma((3,)), dma, dma((6,)), dma, dma((6,)), dma, dma((5,)), dma((6,)), dma((4,)), dma,
             dma((3,)), dma, dma((9,)), dma((9,)), dma((9,)), dma((9,)),
         ],
         compiler_params=pltpu.CompilerParams(
@@ -415,7 +445,9 @@
         out_shape=outs_shape,
         in_specs=[anywhere, anywhere],
         out_specs=(anywhere, anywhere),
-        scratch_shapes=[dma((5,))],
+        scratch_shapes=[
+            pltpu.VMEM((TOK, H * HD), bf16), pltpu.VMEM((1, 4, 1, PAGE, 2 * KVH * HD), bf16), dma((2, 5))
+        ],
     )(*outs)
 
 

time: 111 us -> 69.2 us (0.62)
  Pallas kernels: 110 us -> 68.2 us
    pallas_call x1, Pallas kernels: 40.9 us -> 2.08 us  [per_device(): pl.pallas_call(hand_over, out_shape=outs_shape, in_specs=[anywhere, anywh...]
    pallas_call x1, Pallas kernels: 69.3 us -> 66.1 us  [per_device(): pl.pallas_call(kernel, out_shape=outs_shape, in_specs=[anywhere, anywhere...]
where the time goes in v2:
time: 69.2 us; the launch traced here: 69 us
  Pallas kernels  68.2 us (99%)
  between operations  0.8 us (1%)
    pallas_call x1, Pallas kernels, per_device(): pl.pallas_call(kernel, out_shape=outs_shape, in_specs=[anywhere, anywhere...  66.1 us
    pallas_call x1, Pallas kernels, per_device(): pl.pallas_call(hand_over, out_shape=outs_shape, in_specs=[anywhere, anywh...  2.08 us

profile of v2, /device:TPU:1, one launch (start us, length us, event | category | flops | bytes accessed | tf_op | source)
XLA Modules:
  0.0 69.0 jit_solution(7328172748370432597)
XLA Ops:
  0.6 66.1 %shard_map.68 = (bf16[1,128,4096]{2,1,0:T(8,128)(2,1)}, bf16[1,4,1,32,1024]{4,3,2,1,0:T(8,128)(2,1)}) custom-call(bf16[1,128,4096]{2,1,0:T(8,128)(2,1)} %queries.1, bf16[1,128,1024]{2,1,0:T(8,128)(2,1)} %fresh.1, bf16[4,32,1024]{2,1,0:T(8,128)(2,1)} %pages.1, s32[4,128]{1,0:T(4,128)} %table.1, s32[4]{0:T(128)} %lengths.1), custom_call_target="tpu_custom_call" | custom-call | flops 13958643712 | bytes 4194304 | tf_op jit(solution)/shard_map/pallas_call | solution.py:415
  66.8 2.1 %shard_map.69 = (bf16[1,128,4096]{2,1,0:T(8,128)(2,1)}, bf16[1,4,1,32,1024]{4,3,2,1,0:T(8,128)(2,1)}) custom-call(bf16[1,128,4096]{2,1,0:T(8,128)(2,1)} %get-tuple-element.4.attended_in, bf16[1,4,1,32,1024]{4,3,2,1,0:T(8,128)(2,1)} %get-tuple-element.5.written_in), custom_call_target="tpu_custom_call" | custom-call | tf_op jit(solution)/shard_map/pallas_call | solution.py:443

commit v3 on v2

--- a/solution.py
+++ b/solution.py
@@ -128,7 +128,7 @@
             q_two[i, head * TOK:(head + 1) * TOK, 0:HD] = high
             q_two[i, head * TOK:(head + 1) * TOK, HD:2 * HD] = low
 
-    def prepare_prefix(chunk):
+    def prepare_prefix(chunk, first=0, last=8):
         seen = seen_key[...].astype(jnp.float32)[0:1, :]
         row = lax.broadcasted_iota(jnp.int32, (PAGE, 128), 0).astype(jnp.float32)
 
@@ -145,14 +145,15 @@
                 kvx[2, chunk, b, rows, :] = jnp.where(valid, 1.0, 0.0).astype(jnp.bfloat16)
             return carry
 
-        lax.fori_loop(0, 8, one_block, 0)
-
-    def attend(i, chunk, count, first=False, diagonal=False, blocks=None):
+        lax.fori_loop(first, last, one_block, 0)
+
+    def attend(i, chunk, count, first=False, diagonal=False, blocks=None, half=None):
         blocks = blocks or [(i, slice(r, r + BLOCK)) for r in range(0, ROWS, BLOCK)]
-        width = count * CHUNK
+        width = count * (CHUNK if half is None else CHUNK // 2)
+        part = pl.ds(0, 8) if half is None else pl.ds(half * 4, 4)
 
         def scores(i, rows):
-            key = kvx[0, pl.ds(chunk, count)].reshape(width, HD)
+            key = kvx[0, pl.ds(chunk, count), part].reshape(width, HD)
             two = jnp.concatenate([key, key], axis=1)
             return lax.dot_general(
                 q_two[i, rows, :], two, (((1,), (1,)), ((), ())),
@@ -166,8 +167,7 @@
                 cut = jnp.where(key_at - token <= xc * TOK, s[:, width - CHUNK:], NEG)
                 s = cut if count == 1 else jnp.concatenate([s[:, :width - CHUNK], cut], axis=1)
             value = jnp.concatenate(
-                [kvx[1, pl.ds(chunk, count)].reshape(width, HD), kvx[2, pl.ds(chunk, count)].reshape(width, HD)],
-                axis=1,
+                [kvx[plane, pl.ds(chunk, count), part].reshape(width, HD) for plane in (1, 2)], axis=1
             )
             highest = jnp.max(s, axis=1, keepdims=True)
             if not first:
@@ -239,21 +239,27 @@
         for copy in seen_copies + [own_seen]:
             copy.start()
 
-    for copy in page_copies + q_copies[0::2]:
+    for copy in page_copies + fresh_copies:
         copy.start()
     pltpu.make_async_copy(paged, paged, py_recv).wait()
     for copy in slab_copies + own_slab:
         copy.start()
+    own_new = kvx.at[pl.ds(0, 2), pl.ds(4, 4), xc]
+    pltpu.make_async_copy(own_new, own_new, fr_recv).wait()
+    for name in ("own_r", "own_l", "own_s"):
+        suf_copy(name).start()
     own_slot = raw.at[:, 0, c]
     pltpu.make_async_copy(own_slot, own_slot, pg_recv).wait()
     for name in ("own_r", "own_l", "own_s"):
         pre_copy(name).start()
-    for copy in q_copies[1::2] + fresh_copies:
+    for copy in q_copies[0::2] + q_copies[1::2]:
         copy.start()
     pltpu.make_async_copy(seen_key, seen_key, se_recv).wait()
     pre_copy("own_s").wait_recv()
     prepare_prefix(0)
     up, down = lax.rem(z + 1, 4), lax.rem(z + 3, 4)
+
+    ring = (("own_r", "far_r", "left_s"), ("own_l", "far_l", "right_s"))
 
     def phase_a(k, carry):
         for half in range(2):
@@ -262,66 +268,61 @@
                 wait_queries(up, 1 + half, half)
                 wait_queries(down, 3 + half, half)
 
+        @pl.when(k == 2)
+        def _():
+            for name, far, across in ring:
+                suf_copy(name).wait_recv()
+                suf_copy(far).start()
+                suf_copy(across).start()
+            for copy in [q_far, own_written] + written_copies:
+                copy.start()
+
         blocks = []
         for b in range(4):
             i = jnp.where(k == 0, z, up if b < 2 else down)
             r = jnp.where(k == 0, b * BLOCK, (b % 2) * BLOCK + (k - 1) * HALF)
             blocks.append((i, pl.ds(pl.multiple_of(r, BLOCK), BLOCK)))
         attend(None, 0, 1, first=True, blocks=blocks)
+
         return carry
 
     lax.fori_loop(0, 3, phase_a, 0)
-    pre_copy("own_r").wait_recv()
-    pre_copy("far_r").start()
-    pre_copy("left_s").start()
-    pre_copy("own_l").wait_recv()
-    pre_copy("far_l").start()
-    pre_copy("right_s").start()
-    own_new = kvx.at[pl.ds(0, 2), pl.ds(4, 4), xc]
-    pltpu.make_async_copy(own_new, own_new, fr_recv).wait()
-    for name in ("own_r", "own_l", "own_s"):
-        suf_copy(name).start()
-    for copy in [q_far, own_written] + written_copies:
-        copy.start()
-    pre_copy("left_s").wait_recv()
-    prepare_prefix(1)
-    pre_copy("right_s").wait_recv()
-    prepare_prefix(2)
+    for name, far, across in ring:
+        pre_copy(name).wait_recv()
+        pre_copy(far).start()
+        pre_copy(across).start()
+    prepare_prefix(1, c * 4, c * 4 + 4)
+    prepare_prefix(2, c * 4, c * 4 + 4)
 
     def phase_b(k, carry):
-        @pl.when(k < 2)
-        def _():
-            attend(jnp.where(k == 0, up, down), 1, 2)
+        @pl.when(k != 1)
+        def _():
+            attend(up, 1, 2, half=jnp.where(k == 0, c, 1 - c))
 
         @pl.when(k == 0)
         def _():
-            pre_copy("far_r").wait_recv()
-            pre_copy("fara_s").start()
-            pre_copy("far_l").wait_recv()
-            pre_copy("farb_s").start()
+            other = 4 - c * 4
+            pre_copy("left_s").wait_recv()
+            prepare_prefix(1, other, other + 4)
+            pre_copy("right_s").wait_recv()
+            prepare_prefix(2, other, other + 4)
 
         @pl.when(k == 1)
         def _():
-            suf_copy("own_r").wait_recv()
-            suf_copy("far_r").start()
-            suf_copy("left_s").start()
-            suf_copy("own_l").wait_recv()
-            suf_copy("far_l").start()
-            suf_copy("right_s").start()
-
-        @pl.when(k == 2)
-        def _():
-            i = lax.rem(z + 2, 4)
-            wait_queries(i, 5)
-            attend(i, 0, 3, first=True)
-            suf_copy("far_r").wait_recv()
-            suf_copy("fara_s").start()
-            suf_copy("far_l").wait_recv()
-            suf_copy("farb_s").start()
+            attend(down, 1, 2)
+            for name, across in (("far_r", "fara_s"), ("far_l", "farb_s")):
+                suf_copy(name).wait_recv()
+                suf_copy(across).start()
 
         return carry
 
     lax.fori_loop(0, 3, phase_b, 0)
+    for name, across in (("far_r", "fara_s"), ("far_l", "farb_s")):
+        pre_copy(name).wait_recv()
+        pre_copy(across).start()
+    opposite = lax.rem(z + 2, 4)
+    wait_queries(opposite, 5)
+    attend(opposite, 0, 3, first=True)
     for name in ("fara_s", "farb_s"):
         pre_copy(name).wait_recv()
     prepare_prefix(3)
@@ -383,6 +384,7 @@
 
     for name in pre_plan:
         pre_copy(name).wait_send()
+    for name in suf_plan:
         suf_copy(name).wait_send()
     pltpu.make_async_copy(written, written, np_recv).wait()
     for dz in (1, 3, 2):

time: 69.2 us -> 65.1 us (0.941)
  Pallas kernels: 68.2 us -> 64.1 us
    pallas_call x1, Pallas kernels: 66.1 us -> 62 us  [per_device(): pl.pallas_call(kernel, out_shape=outs_shape, in_specs=[anywhere, anywhere...]
where the time goes in v3:
time: 65.1 us; the launch traced here: 64.9 us
  Pallas kernels  64.1 us (98%)
  between operations  0.8 us (1%)
    pallas_call x1, Pallas kernels, per_device(): pl.pallas_call(kernel, out_shape=outs_shape, in_specs=[anywhere, anywhere...  62 us
    pallas_call x1, Pallas kernels, per_device(): pl.pallas_call(hand_over, out_shape=outs_shape, in_specs=[anywhere, anywh...  2.08 us

profile of v3, /device:TPU:1, one launch (start us, length us, event | category | flops | bytes accessed | tf_op | source)
XLA Modules:
  0.0 64.9 jit_solution(5407803142887360113)
XLA Ops:
  0.6 62.0 %shard_map.68 = (bf16[1,128,4096]{2,1,0:T(8,128)(2,1)}, bf16[1,4,1,32,1024]{4,3,2,1,0:T(8,128)(2,1)}) custom-call(bf16[1,128,4096]{2,1,0:T(8,128)(2,1)} %queries.1, bf16[1,128,1024]{2,1,0:T(8,128)(2,1)} %fresh.1, bf16[4,32,1024]{2,1,0:T(8,128)(2,1)} %pages.1, s32[4,128]{1,0:T(4,128)} %table.1, s32[4]{0:T(128)} %lengths.1), custom_call_target="tpu_custom_call" | custom-call | flops 13958643712 | bytes 4194304 | tf_op jit(solution)/shard_map/pallas_call | solution.py:417
  62.7 2.1 %shard_map.69 = (bf16[1,128,4096]{2,1,0:T(8,128)(2,1)}, bf16[1,4,1,32,1024]{4,3,2,1,0:T(8,128)(2,1)}) custom-call(bf16[1,128,4096]{2,1,0:T(8,128)(2,1)} %get-tuple-element.4.attended_in, bf16[1,4,1,32,1024]{4,3,2,1,0:T(8,128)(2,1)} %get-tuple-element.5.written_in), custom_call_target="tpu_custom_call" | custom-call | tf_op jit(solution)/shard_map/pallas_call | solution.py:445
